TPU v7x, 32 devices: a whole 2x2x4 slice. The times are simulated.
32 devices in a mesh: feat: 4 (over z), img: 8 (over y, x, core).
Axes of the slice: x: 2, y: 2, z: 4, core: 2. Of those that a mesh axis runs over, the one named last changes fastest.
Arguments:
- features: bfloat16 [448, 61440], P('img', 'feat'), may hold values from -6 to 6
- proj_in: bfloat16 [61440, 768], P('feat', 'img'), may hold values from -0.0234375 to 0.0234375
- proj_out: bfloat16 [768, 512], P('feat'), may hold values from -0.21875 to 0.21875
- centres: bfloat16 [16384, 512], P(('feat', 'img')), may hold values from -0.25 to 0.25
- labels: int32 [448], P('img'), may hold values from 0 to 16383
Outputs:
- centre_grad: float32 [16384, 512], P(('feat', 'img'))
- emb_grad: float32 [448, 512], P('img', 'feat')
Inputs may be any that keep to these rules, and one draw needn't show every extreme that they name: `labels`: each image's identity is among the sampled centres, at this position.
All inputs are finite; a program needn't handle non-finite values.
Results may differ from a plain program's by a relative error of at most 0.006.
Values may be sent and summed in bfloat16 or wider, within the bound.
A program may use at most 64 MiB of HBM per device.

v0:
```python
import jax
import jax.numpy as jnp
from jax import lax
from jax.sharding import PartitionSpec as P

norm_eps = 1e-06
scale_logit = 64.0
margin_angle = 0.5
sine_floor = 0.04


def per_device(features, proj_in, proj_out, centres, labels):
    emb_width = proj_out.shape[1]
    local_cols = jnp.dot(
        lax.all_gather(features, "img", axis=0, tiled=True),
        proj_in,
        preferred_element_type=jnp.float32,
    )
    partial_hidden = lax.all_to_all(local_cols, "img", split_axis=0, concat_axis=1, tiled=True)
    hidden = lax.psum(partial_hidden, "feat").astype(jnp.bfloat16)
    embed = jnp.dot(
        hidden,
        lax.all_gather(proj_out, "feat", axis=0, tiled=True),
        preferred_element_type=jnp.float32,
    )
    inverse = lax.rsqrt(jnp.sum(embed * embed, axis=1) + norm_eps)
    unit = embed * inverse[:, None]
    unit_low = unit.astype(jnp.bfloat16)
    all_units, all_labels = (
        lax.all_gather(unit_low, "img", axis=0, tiled=True),
        lax.all_gather(labels, "img", axis=0, tiled=True),
    )
    cen_rows = centres.shape[0]
    wide = centres.astype(jnp.float32)
    cinv = lax.rsqrt(jnp.sum(wide * wide, axis=1) + norm_eps)
    unit_centre = wide * cinv[:, None]
    centre_low = unit_centre.astype(jnp.bfloat16)
    cosine = jnp.dot(all_units, centre_low.T, preferred_element_type=jnp.float32)
    begin = lax.axis_index(("feat", "img")) * cen_rows
    position = begin + jnp.arange(cen_rows, dtype=jnp.int32)
    target = all_labels[:, None] == position[None, :]
    cos_m = jnp.cos(jnp.float32(margin_angle))
    sin_m = jnp.sin(jnp.float32(margin_angle))
    inner = 1.0 - cosine * cosine
    sine = jnp.sqrt(jnp.maximum(inner, sine_floor))
    logit = jnp.where(target, scale_logit * (cosine * cos_m - sine * sin_m), scale_logit * cosine)
    exps = jnp.exp(logit)
    total = lax.psum(jnp.sum(exps, axis=1), ("feat", "img"))
    dlogit = exps / total[:, None] - target.astype(jnp.float32)
    slope = cos_m + jnp.where(inner > sine_floor, sin_m * cosine / sine, 0.0)
    dcos = (dlogit * scale_logit * jnp.where(target, slope, 1.0)).astype(jnp.bfloat16)
    gunit = jnp.dot(dcos.T, all_units, preferred_element_type=jnp.float32)
    centre_grad = cinv[:, None] * (
        gunit - unit_centre * jnp.sum(unit_centre * gunit, axis=1, keepdims=True)
    )
    dunit_terms = jnp.dot(dcos, centre_low, preferred_element_type=jnp.float32)
    slice_width = emb_width // lax.axis_size("feat")
    col_start = lax.axis_index("feat") * slice_width
    row_sums = lax.psum_scatter(dunit_terms, "img", scatter_dimension=0, tiled=True)
    dunit = lax.psum(row_sums, "feat")
    full_grad = inverse[:, None] * (dunit - unit * jnp.sum(unit * dunit, axis=1, keepdims=True))
    emb_grad = lax.dynamic_slice_in_dim(full_grad, col_start, slice_width, 1)
    return (centre_grad, emb_grad)


def solution(mesh):
    return jax.shard_map(
        per_device,
        mesh=mesh,
        in_specs=(
            P("img", "feat"),
            P("feat", "img"),
            P("feat", None),
            P(("feat", "img"), None),
            P("img"),
        ),
        out_specs=(P(("feat", "img"), None), P("img", "feat")),
        check_vma=False,
    )
```

profile of v0, /device:TPU:0, one launch (start us, length us, event | category | flops | bytes accessed | tf_op | source)
XLA Modules:
  0.0 274.8 jit_solution(6855363726423225952)
XLA Ops:
  7.2 0.0 all-gather.2.cloned.1.call-start
  7.2 0.7 all-gather.2.cloned.1.call-update
  7.9 1.4 copy.9
  9.3 0.2 fusion.6
  9.5 21.7 %all_gather.14 = bf16[768,512]{1,0:T(8,128)(2,1)} all-gather(bf16[192,512]{1,0:T(8,128)(2,1)} %param.7), channel_id=1, replica_groups=mesh['feat'=4,'img'=8] {'feat'}, dimensions={0}, use_global_device_ids=true | all-gather | bytes 983040 | tf_op jit(solution)/shard_map/all_gather | solution.py:23
  31.2 58.6 %all-gather.2.cloned.1.call-done = bf16[448,15360]{1,0:T(8,128)(2,1)} async-done(((bf16[56,15360]{1,0:T(8,128)(2,1)}), bf16[448,15360]{1,0:T(8,128)(2,1)}) %all-gather.2.cloned.1.call-update) | async-done | bytes 13762576 | tf_op jit(solution)/shard_map/all_gather | solution.py:15
  89.8 7.5 %fusion.21 = f32[448,96]{1,0:T(8,128)} fusion(bf16[448,15360]{1,0:T(8,128)(2,1)} %all-gather.2.cloned.1.call-done, bf16[15360,96]{0,1:T(8,128)(2,1)S(1)} %copy-done), kind=kOutput, calls=%fused_computation.34 | convolution fusion | flops 1321205760 | bytes 16883712 | tf_op jit(solution)/shard_map/dot_general | solution.py:14
  97.3 4.0 %all-to-all-start = ((f32[8,56,96]{2,1,0:T(8,128)}), f32[8,56,96]{2,1,0:T(8,128)}, u32[]{:S(2)}, u32[]{:S(2)}) async-start(f32[8,56,96]{2,1,0:T(8,128)} %bitcast.11), calls=%async_computation | async-start | bytes 458752 | tf_op jit(solution)/shard_map/all_to_all | solution.py:19
  101.3 0.0 reduce-scatter.2.cloned.1.call-start
  101.4 0.6 dynamic-slice
  102.7 0.2 dynamic-update-slice
  102.9 8.3 %all-reduce = s32[448]{0:T(512)S(1)} all-reduce(s32[448]{0:T(512)S(1)} %dynamic-update-slice), channel_id=1, replica_groups=mesh['feat'=4,'img'=8] {'img'}, use_global_device_ids=true, to_apply=%add | all-reduce | flops 448 | bytes 3584
  111.2 1.7 copy.11
  112.9 1.7 all_to_all.17
  114.6 22.8 %all-reduce.5 = bf16[56,768]{1,0:T(8,128)(2,1)} all-reduce(f32[56,768]{1,0:T(8,128)} %all_to_all.17), channel_id=1, replica_groups=mesh['feat'=4,'img'=8] {'feat'}, use_global_device_ids=true, to_apply=%region_1.0 | all-reduce | flops 43008 | bytes 258048 | tf_op jit(solution)/shard_map/psum | solution.py:20
  137.4 1.5 multiply_reduce_fusion.1
  138.9 0.7 fusion.20
  139.7 9.1 %all_gather.15 = bf16[448,512]{1,0:T(8,128)(2,1)S(1)} all-gather(bf16[56,512]{1,0:T(8,128)(2,1)S(1)} %get-tuple-element.6), channel_id=1, replica_groups=mesh['feat'=4,'img'=8] {'img'}, dimensions={0}, use_global_device_ids=true | all-gather | bytes 516096 | tf_op jit(solution)/shard_map/all_gather | solution.py:30
  148.8 0.8 copy-done.2
  149.6 1.8 fusion.12
  151.4 37.6 %psum.22 = f32[448]{0:T(512)S(1)} all-reduce(f32[448]{0:T(512)S(1)} %get-tuple-element.10), channel_id=1, replica_groups=mesh['feat'=4,'img'=8] {'feat','img'}, use_global_device_ids=true, to_apply=%region_4.5 | all-reduce | flops 448 | bytes 3584 | tf_op jit(solution)/shard_map/psum | solution.py:48
  189.0 2.1 fusion.11
  191.2 0.8 copy-done.1
  192.0 1.4 fusion.13
  193.4 0.0 all-reduce.4.cloned.1.call-start
  193.4 2.6 fusion.3
  196.0 33.3 %reduce-scatter.2.cloned.1.call-done = f32[56,512]{1,0:T(8,128)} async-done(((f32[448,512]{1,0:T(8,128)}), f32[56,512]{1,0:T(8,128)}) %reduce-scatter.2.cloned.1.call-update) | async-done | bytes 114704 | tf_op jit(solution)/shard_map/reduce_scatter | solution.py:59
  229.3 2.4 fusion.5
  231.8 2.5 copy.12
  234.3 31.5 %all-reduce.4.cloned.1.call-done = f32[56,512]{1,0:T(8,128)} async-done(((f32[56,512]{1,0:T(8,128)}), f32[56,512]{1,0:T(8,128)}) %all-reduce.4.cloned.1.call-update) | async-done | bytes 114704 | tf_op jit(solution)/shard_map/psum | solution.py:60
  265.8 1.1 multiply_reduce_fusion
  266.8 1.5 fusion.19
  (15 shorter events, 0.1 us)
Async XLA Ops:
  7.2 82.6 %copy-start = (bf16[15360,96]{0,1:T(8,128)(2,1)S(1)}, bf16[15360,96]{0,1:T(8,128)(2,1)}, u32[]{:S(2)}) copy-start(bf16[15360,96]{0,1:T(8,128)(2,1)} %param.6) | copy-start | bytes 8847364
  7.2 82.6 %all-gather.2.cloned.1.call-start = ((), (), s32[]{:S(2)}) async-start(), calls=%async_computation.2 | async-start | bytes 15482880 | tf_op jit(solution)/shard_map/all_gather | solution.py:15
  31.2 70.2 %copy-start.4 = (u32[32]{0:T(128)S(1)}, u32[32]{0:T(128)}, u32[]{:S(2)}) copy-start(u32[32]{0:T(128)} %constant.34) | copy-start | bytes 388
  31.2 71.5 %copy-start.3 = (s32[56]{0:T(128)S(1)}, s32[56]{0:T(128)}, u32[]{:S(2)}) copy-start(s32[56]{0:T(128)} %param.9) | copy-start | bytes 676
  97.3 14.0 %all-to-all-start = ((f32[8,56,96]{2,1,0:T(8,128)}), f32[8,56,96]{2,1,0:T(8,128)}, u32[]{:S(2)}, u32[]{:S(2)}) async-start(f32[8,56,96]{2,1,0:T(8,128)} %bitcast.11), calls=%async_computation | async-start | bytes 458752 | tf_op jit(solution)/shard_map/all_to_all | solution.py:19
  101.3 128.0 %reduce-scatter.2.cloned.1.call-start = ((), (), s32[]{:S(2)}) async-start(), calls=%async_computation.3 | async-start | bytes 1032192 | tf_op jit(solution)/shard_map/reduce_scatter | solution.py:59
  148.8 0.8 copy-start.2
  191.2 0.8 copy-start.1
  193.4 72.4 %all-reduce.4.cloned.1.call-start = ((), (), s32[]{:S(2)}) async-start(), calls=%async_computation.4 | async-start | bytes 229376 | tf_op jit(solution)/shard_map/psum | solution.py:60
Sparse Core Ops, SparseCore 0:
  9.9 79.7 all-gather.1
  193.5 35.7 reduce-scatter.1
  231.6 34.0 all-reduce.3
where the time goes:
time: 276 us; the launch traced here: 275 us
  waiting for transfers between devices  124 us (45%)
  blocking collectives  99.5 us (36%)
  matrix products  14.9 us (5%)
  between operations  14.5 us (5%)
  local copies, waits for them, and re-layouts  9.73 us (4%)
  other arithmetic  7.98 us (3%)
  starting transfers between devices  4.15 us (2%)
    all_gather x1, waiting for transfers between devices, per_device(): lax.all_gather(features, 'img', axis=0, tiled=True)  58.6 us
    psum x1, blocking collectives, per_device(): total = lax.psum(jnp.sum(exps, axis=1), ('feat', 'img'))  37.6 us
    reduce_scatter x1, waiting for transfers between devices, per_device(): lax.psum_scatter(dunit_terms, 'img', scatter_dimension=0, tiled=True)  33.3 us
    psum x1, waiting for transfers between devices, per_device(): dunit = lax.psum(row_sums, 'feat')  31.5 us
    psum x1, blocking collectives, per_device(): hidden = lax.psum(partial_hidden, 'feat').astype(jnp.bfloat16)  22.8 us
    all_gather x1, blocking collectives, per_device(): lax.all_gather(proj_out, 'feat', axis=0, tiled=True)  21.7 us
    all_gather x1, blocking collectives, per_device(): lax.all_gather(unit_low, 'img', axis=0, tiled=True)  9.09 us
    unnamed x1, blocking collectives  8.34 us
  transfers between devices with their start and end apart: 4, of which 3 were waited for; matrix products, arithmetic and copies ran while one was open for 4% of the time, Pallas kernels for 0%

commit v1 on v0

v1 whole, which is shorter than its diff:
```python
import functools

import jax
import jax.numpy as jnp
from jax import lax
from jax.experimental import pallas as pl
from jax.experimental.pallas import tpu as pltpu
from jax.sharding import PartitionSpec as P

norm_eps = 1e-06
scale_logit = 64.0
margin_angle = 0.5
sine_floor = 0.04
MESH = pl.DeviceIdType.MESH


def remote(src, dst, send, recv, axis, peer):
    return pltpu.make_async_remote_copy(
        src_ref=src, dst_ref=dst, send_sem=send, recv_sem=recv, device_id={axis: peer}, device_id_type=MESH
    )


def tail(nf, ni, p_ref, po_ref, cen_ref, lab_ref, trig_ref, cg_ref, eg_ref,
         z1, h, lab, u, emb, eo, clow, cosb, tp, tz, msg, rs, zs, zr, uq,
         s1, r1, s2, r2, sl, rl, s4, r4, se, re, s5, r5, s6, r6, s7, r7, s8, r8):
    f, j = lax.axis_index("feat"), lax.axis_index("img")
    images, cols = p_ref.shape
    rows = images // nf
    own = images // ni
    width = cen_ref.shape[1]
    part = width // nf
    zpeer = lambda d: lax.rem(f + d, nf)
    ipeer = lambda d: lax.rem(j + d, ni)

    barrier = pltpu.get_barrier_semaphore()
    for d in range(1, ni):
        pl.semaphore_signal(barrier, inc=1, device_id={"img": ipeer(d)}, device_id_type=MESH)
    for d in range(1, nf):
        pl.semaphore_signal(barrier, inc=1, device_id={"feat": zpeer(d)}, device_id_type=MESH)
    pl.semaphore_wait(barrier, ni + nf - 2)

    sent = []

    def to_feat(src, dst, s, r):
        out = []
        for d in range(1, nf):
            c = remote(src(zpeer(d)), dst(d), s.at[d], r.at[d], "feat", zpeer(d))
            c.start()
            out.append(c)
        sent.extend(out)
        return out

    def to_img(src, dst, s, r):
        out = []
        for d in range(1, ni):
            c = remote(src(ipeer(d)), dst(d), s.at[d], r.at[d], "img", ipeer(d))
            c.start()
            out.append(c)
        sent.extend(out)
        return out

    first = to_feat(lambda g: p_ref.at[pl.ds(pl.multiple_of(g * rows, rows), rows)], lambda d: z1.at[d], s1, r1)
    labs = to_img(lambda c: lab_ref, lambda d: lab.at[d], sl, rl)
    wide = cen_ref[...].astype(jnp.float32)
    cinv = lax.rsqrt(jnp.sum(wide * wide, axis=1, keepdims=True) + norm_eps)
    clow[...] = (wide * cinv).astype(jnp.bfloat16)
    hid = p_ref[pl.ds(pl.multiple_of(f * rows, rows), rows)]
    for d in range(1, nf):
        first[d - 1].wait_recv()
        hid = hid + z1[d]
    h[0] = hid.astype(jnp.bfloat16)

    for c in to_img(lambda c: h.at[0], lambda d: h.at[d], s2, r2):
        c.wait_recv()
    embed = jnp.zeros((rows, width), jnp.float32)
    for c in range(ni):
        slot = lax.rem(j - c + ni, ni)
        embed = embed + jnp.dot(h[slot], po_ref[c], preferred_element_type=jnp.float32)
    emb[...] = embed
    inverse = lax.rsqrt(jnp.sum(embed * embed, axis=1, keepdims=True) + norm_eps)
    u[f] = (embed * inverse).astype(jnp.bfloat16)

    units = to_feat(lambda g: u.at[f], lambda d: u.at[f], s4, r4)
    holder = (j * own) // rows
    offset = pl.multiple_of(lax.rem(j * own, rows), own)
    home = f == holder

    @pl.when(home)
    def _():
        for d in range(1, nf):
            remote(emb.at[pl.ds(offset, own)], eo, se.at[d], re, "feat", zpeer(d)).start()
        eo[...] = emb[pl.ds(offset, own)]

    for d in range(1, nf):
        back = lax.rem(f - d + nf, nf)
        remote(u.at[back], u.at[back], s4.at[d], r4.at[d], "feat", zpeer(d)).wait_recv()
    for c in labs:
        c.wait_recv()
    label = lab_ref[...]
    for d in range(1, ni):
        label = label + lab[d]
    label = label[:1]

    allu = u[...].reshape(images, width)
    cosine = lax.dot_general(clow[...], allu, (((1,), (1,)), ((), ())), preferred_element_type=jnp.float32)
    cen_rows = cen_ref.shape[0]
    begin = (f * ni + j) * cen_rows
    cos_m, sin_m = trig_ref[0], trig_ref[1]

    def forms(cosine):
        position = begin + lax.broadcasted_iota(jnp.int32, cosine.shape, 0)
        target = position == label
        inner = 1.0 - cosine * cosine
        sine = jnp.sqrt(jnp.maximum(inner, sine_floor))
        return target, inner, sine

    target, inner, sine = forms(cosine)
    logit = jnp.where(target, scale_logit * (cosine * cos_m - sine * sin_m), scale_logit * cosine)
    exps = jnp.exp(logit)
    cosb[...] = cosine
    tp[0] = jnp.sum(exps, axis=0, keepdims=True)
    total = tp[0]
    for d, c in enumerate(to_img(lambda c: tp.at[0], lambda d: tp.at[d], s5, r5), 1):
        c.wait_recv()
        total = total + tp[d]
    tz[0] = total
    for d, c in enumerate(to_feat(lambda g: tz.at[0], lambda d: tz.at[d], s6, r6), 1):
        c.wait_recv()
        total = total + tz[d]

    cosine = cosb[...]
    target, inner, sine = forms(cosine)
    logit = jnp.where(target, scale_logit * (cosine * cos_m - sine * sin_m), scale_logit * cosine)
    dlogit = jnp.exp(logit) / total - target.astype(jnp.float32)
    slope = cos_m + jnp.where(inner > sine_floor, sin_m * cosine / sine, 0.0)
    dcos = (dlogit * scale_logit * jnp.where(target, slope, 1.0)).astype(jnp.bfloat16)

    terms = lax.dot_general(dcos, clow[...], (((0,), (0,)), ((), ())), preferred_element_type=jnp.float32)
    half = width // 2
    for c in range(ni):
        block = terms[c * own:(c + 1) * own]
        msg[c] = jnp.concatenate([block[:, :half], block[:, half:]], axis=0).astype(jnp.bfloat16)
    scatter = to_img(lambda c: msg.at[c], lambda d: rs.at[d], s7, r7)

    gunit = jnp.dot(dcos, allu, preferred_element_type=jnp.float32)
    wide = cen_ref[...].astype(jnp.float32)
    cinv = lax.rsqrt(jnp.sum(wide * wide, axis=1, keepdims=True) + norm_eps)
    unit_centre = wide * cinv
    cg_ref[...] = cinv * (gunit - unit_centre * jnp.sum(unit_centre * gunit, axis=1, keepdims=True))

    @pl.when(jnp.logical_not(home))
    def _():
        remote(eo, eo, se.at[0], re, "feat", zpeer(1)).wait_recv()

    mine = eo[...]
    inverse = lax.rsqrt(jnp.sum(mine * mine, axis=1, keepdims=True) + norm_eps)
    unit = mine * inverse
    for g in range(nf):
        uq[g] = unit[:, g * part:(g + 1) * part]
    packed = msg[j].astype(jnp.float32)
    for d in range(1, ni):
        scatter[d - 1].wait_recv()
        packed = packed + rs[d].astype(jnp.float32)
    sums = jnp.concatenate([packed[:own], packed[own:]], axis=1)
    along = jnp.sum(unit * sums, axis=1, keepdims=True)
    for g in range(nf):
        zs[g, :own] = sums[:, g * part:(g + 1) * part]
        zs[g, own:] = jnp.broadcast_to(along, (own, part))
    final = zs[f]
    for d, c in enumerate(to_feat(lambda g: zs.at[g], lambda d: zr.at[d], s8, r8), 1):
        c.wait_recv()
        final = final + zr[d]
    eg_ref[...] = inverse * (final[:own] - uq[f] * final[own:])

    for c in sent:
        c.wait_send()

    @pl.when(home)
    def _():
        for d in range(1, nf):
            remote(emb.at[pl.ds(offset, own)], eo, se.at[d], re, "feat", zpeer(d)).wait_send()


def run_tail(nf, ni, local_cols, all_out, centres, lab_rows, trig):
    images, cols = local_cols.shape
    cen_rows, width = centres.shape
    rows, own, part = images // nf, images // ni, width // nf
    f32, bf16 = jnp.float32, jnp.bfloat16
    dma = pltpu.SemaphoreType.DMA
    vm = pl.BlockSpec(memory_space=pltpu.VMEM)
    return pl.pallas_call(
        functools.partial(tail, nf, ni),
        out_shape=(
            jax.ShapeDtypeStruct((cen_rows, width), f32),
            jax.ShapeDtypeStruct((own, part), f32),
        ),
        in_specs=[vm, vm, vm, vm, pl.BlockSpec(memory_space=pltpu.SMEM)],
        out_specs=(vm, vm),
        scratch_shapes=[
            pltpu.VMEM((nf, rows, cols), f32),
            pltpu.VMEM((ni, rows, cols), bf16),
            pltpu.VMEM((ni,) + lab_rows.shape, jnp.int32),
            pltpu.VMEM((nf, rows, width), bf16),
            pltpu.VMEM((rows, width), f32),
            pltpu.VMEM((own, width), f32),
            pltpu.VMEM((cen_rows, width), bf16),
            pltpu.VMEM((cen_rows, images), f32),
            pltpu.VMEM((ni, 1, images), f32),
            pltpu.VMEM((nf, 1, images), f32),
            pltpu.VMEM((ni, 2 * own, width // 2), bf16),
            pltpu.VMEM((ni, 2 * own, width // 2), bf16),
            pltpu.VMEM((nf, 2 * own, part), f32),
            pltpu.VMEM((nf, 2 * own, part), f32),
            pltpu.VMEM((nf, own, part), f32),
            dma((nf,)), dma((nf,)),
            dma((ni,)), dma((ni,)),
            dma((ni,)), dma((ni,)),
            dma((nf,)), dma((nf,)),
            dma((nf,)), dma(()),
            dma((ni,)), dma((ni,)),
            dma((nf,)), dma((nf,)),
            dma((ni,)), dma((ni,)),
            dma((nf,)), dma((nf,)),
        ],
        compiler_params=pltpu.CompilerParams(
            collective_id=1, has_side_effects=True, vmem_limit_bytes=48 * 1024 * 1024
        ),
    )(local_cols, all_out, centres, lab_rows, trig)


def per_device(features, proj_in, proj_out, centres, labels):
    nf, ni = lax.axis_size("feat"), lax.axis_size("img")
    own = labels.shape[0]
    local_cols = jnp.dot(
        lax.all_gather(features, "img", axis=0, tiled=True),
        proj_in,
        preferred_element_type=jnp.float32,
    )
    all_out = lax.all_gather(proj_out, "feat", axis=0, tiled=True)
    all_out = all_out.reshape(ni, all_out.shape[0] // ni, all_out.shape[1])
    lab_row = lax.dynamic_update_slice(
        jnp.zeros((own * ni,), jnp.int32), labels, (lax.axis_index("img") * own,)
    )
    lab_rows = jnp.broadcast_to(lab_row[None], (8, own * ni))
    trig = jnp.stack([jnp.cos(jnp.float32(margin_angle)), jnp.sin(jnp.float32(margin_angle))])
    return run_tail(nf, ni, local_cols, all_out, centres, lab_rows, trig)


def solution(mesh):
    return jax.shard_map(
        per_device,
        mesh=mesh,
        in_specs=(
            P("img", "feat"),
            P("feat", "img"),
            P("feat", None),
            P(("feat", "img"), None),
            P("img"),
        ),
        out_specs=(P(("feat", "img"), None), P("img", "feat")),
        check_vma=False,
    )
```

time: 276 us -> 157 us (0.57)
  blocking collectives: 99.5 us -> 21.8 us
  waiting for transfers between devices: 124 us -> 59.7 us
  Pallas kernels: 0 us -> 51.4 us
  matrix products: 14.9 us -> 6.92 us
  other arithmetic: 7.98 us -> 0 us
  local copies, waits for them, and re-layouts: 9.73 us -> 2.57 us
  starting transfers between devices: 4.15 us -> 0.04 us
    psum x2 -> x0, blocking collectives: 60.4 us -> none  [the longest x1 37.6 us: per_device(): total = lax.psum(jnp.sum(exps, axis=1), ('feat', 'img'))]
    pallas_call x0 -> x1, Pallas kernels: none -> 51.4 us  [run_tail(): pl.pallas_call(functools.partial(tail, nf, ni), out_shape=(jax.ShapeDtype...]
    reduce_scatter x1 -> x0, waiting for transfers between devices: 33.3 us -> none  [per_device(): lax.psum_scatter(dunit_terms, 'img', scatter_dimension=0, tiled=True)]
    psum x1 -> x0, waiting for transfers between devices: 31.5 us -> none  [per_device(): dunit = lax.psum(row_sums, 'feat')]
    all_gather x2 -> x1, blocking collectives: 30.8 us -> 21.8 us  [per_device(): all_out = lax.all_gather(proj_out, 'feat', axis=0, tiled=True)]
    unnamed x1 -> x0, blocking collectives: 8.34 us -> none
    dot_general x4 -> x0, matrix products: 7.35 us -> none  [the longest x1 2.62 us: per_device(): gunit = jnp.dot(dcos.T, all_units, preferred_element_type=jnp.float32)]
    unnamed x15 -> x10, local copies, waits for them, and re-layouts: 6.35 us -> 1.6 us
  transfers between devices with their start and end apart: 4 -> 1, of which waited for: 3 -> 1; matrix products, arithmetic and copies ran while one was open for 4% -> 1% of each run, Pallas kernels for 0% -> 0%
where the time goes in v1:
time: 157 us
  waiting for transfers between devices  59.7 us (38%)
  Pallas kernels  51.4 us (33%)
  blocking collectives  21.8 us (14%)
  between operations  14.1 us (9%)
  matrix products  6.92 us (4%)
  local copies, waits for them, and re-layouts  2.57 us (2%)
    all_gather x1, waiting for transfers between devices, per_device(): lax.all_gather(features, 'img', axis=0, tiled=True)  59.1 us
    pallas_call x1, Pallas kernels, run_tail(): pl.pallas_call(functools.partial(tail, nf, ni), out_shape=(jax.ShapeDtype...  51.4 us
    all_gather x1, blocking collectives, per_device(): all_out = lax.all_gather(proj_out, 'feat', axis=0, tiled=True)  21.8 us
    dot_general x1, matrix products, per_device(): jnp.dot(lax.all_gather(features, 'img', axis=0, tiled=True), proj_in, pre...  6.92 us
  transfers between devices with their start and end apart: 1, of which 1 were waited for; matrix products, arithmetic and copies ran while one was open for 1% of the time, Pallas kernels for 0%

profile of v1, /device:TPU:0, one launch (start us, length us, event | category | flops | bytes accessed | tf_op | source)
XLA Modules:
  0.0 156.5 jit_solution(6140458629316936530)
XLA Ops:
  7.2 0.0 copy-start
  7.2 0.0 all-gather.2.cloned.1.call-start
  7.2 0.7 all-gather.2.cloned.1.call-update
  7.9 1.0 dynamic_update_slice.5
  8.9 21.8 %all_gather.7 = bf16[768,512]{1,0:T(8,128)(2,1)} all-gather(bf16[192,512]{1,0:T(8,128)(2,1)} %param.7), channel_id=1, replica_groups=mesh['feat'=4,'img'=8] {'feat'}, dimensions={0}, use_global_device_ids=true | all-gather | bytes 983040 | tf_op jit(solution)/shard_map/all_gather | solution.py:239
  30.7 0.0 copy-start.2
  30.7 0.0 copy-start.3
  30.7 59.1 %all-gather.2.cloned.1.call-done = bf16[448,15360]{1,0:T(8,128)(2,1)} async-done(((bf16[56,15360]{1,0:T(8,128)(2,1)}), bf16[448,15360]{1,0:T(8,128)(2,1)}) %all-gather.2.cloned.1.call-update) | async-done | bytes 13762576 | tf_op jit(solution)/shard_map/all_gather | solution.py:235
  89.8 0.0 copy-done
  89.8 0.0 copy-start.1
  89.8 6.9 %fusion.p_ref = f32[448,96]{1,0:T(8,128)S(1)} fusion(bf16[448,15360]{1,0:T(8,128)(2,1)} %all-gather.2.cloned.1.call-done, bf16[15360,96]{0,1:T(8,128)(2,1)S(1)} %copy-done), kind=kOutput, calls=%fused_computation | convolution fusion | flops 1321205760 | bytes 16883712 | tf_op jit(solution)/shard_map/dot_general | solution.py:234
  96.7 0.0 copy-done.2
  96.7 0.0 copy-done.3
  96.7 0.0 copy-done.1
  96.7 51.4 %shard_map.68 = (f32[512,512]{1,0:T(8,128)S(1)}, f32[56,128]{1,0:T(8,128)S(1)}) custom-call(f32[448,96]{1,0:T(8,128)S(1)} %fusion.p_ref, bf16[8,96,512]{2,1,0:T(8,128)(2,1)S(1)} %bitcast.3, bf16[512,512]{1,0:T(8,128)(2,1)S(1)} %copy-done.2, s32[8,448]{1,0:T(8,128)S(1)} %broadcast_in_dim.10.lab_ref, f32[2]{0:T(128)S(1)} %copy-done.3), custom_call_target="tpu_custom_call" | custom-call | tf_op jit(solution)/shard_map/pallas_call | solution.py:191
  148.1 1.0 copy.12
  149.1 0.6 copy.13
  (2 shorter events, 0.0 us)
Async XLA Ops:
  7.2 82.6 %copy-start = (bf16[15360,96]{0,1:T(8,128)(2,1)S(1)}, bf16[15360,96]{0,1:T(8,128)(2,1)}, u32[]{:S(2)}) copy-start(bf16[15360,96]{0,1:T(8,128)(2,1)} %param.6) | copy-start | bytes 8847364
  7.2 82.6 %all-gather.2.cloned.1.call-start = ((), (), s32[]{:S(2)}) async-start(), calls=%async_computation | async-start | bytes 15482880 | tf_op jit(solution)/shard_map/all_gather | solution.py:235
  30.7 66.0 %copy-start.2 = (bf16[512,512]{1,0:T(8,128)(2,1)S(1)}, bf16[512,512]{1,0:T(8,128)(2,1)}, u32[]{:S(2)}) copy-start(bf16[512,512]{1,0:T(8,128)(2,1)} %cen_ref.1) | copy-start | bytes 1572868
  30.7 66.0 %copy-start.3 = (f32[2]{0:T(128)S(1)}, f32[2]{0:T(128)}, u32[]{:S(2)}) copy-start(f32[2]{0:T(128)} %constant.14.clone.1.trig_ref) | copy-start | bytes 28
  89.8 7.0 %copy-start.1 = (bf16[768,512]{1,0:T(8,128)(2,1)S(1)}, bf16[768,512]{1,0:T(8,128)(2,1)}, u32[]{:S(2)}) copy-start(bf16[768,512]{1,0:T(8,128)(2,1)} %all_gather.7) | copy-start | bytes 2359300
Sparse Core Ops, SparseCore 0:
  9.9 79.8 all-gather.1

commit v2 on v1

--- a/solution.py
+++ b/solution.py
@@ -1,4 +1,5 @@
 import functools
+import math
 
 import jax
 import jax.numpy as jnp
@@ -20,9 +21,95 @@
     )
 
 
-def tail(nf, ni, p_ref, po_ref, cen_ref, lab_ref, trig_ref, cg_ref, eg_ref,
-         z1, h, lab, u, emb, eo, clow, cosb, tp, tz, msg, rs, zs, zr, uq,
-         s1, r1, s2, r2, sl, rl, s4, r4, se, re, s5, r5, s6, r6, s7, r7, s8, r8):
+def gather_project(core_j, ni, feat_ref, pin_ref, p_ref, g, b, own_sem, b_sem, sends, recvs, compute):
+    j = core_j
+    count, _, own, w = g.shape
+    mid = count // 2
+    core, x, y = lax.rem(j, 2), lax.rem(j // 2, 2), j // 4
+    to_s, to_x, to_y = 1 - 2 * core, 2 - 4 * x, 4 - 8 * y
+    js, jx, jy = j + to_s, j + to_x, j + to_y
+    jd = jx + to_y
+
+    bcopy = pltpu.make_async_copy(pin_ref, b, b_sem)
+    bcopy.start()
+    cols = lambda k: feat_ref.at[:, k * w:(k + 1) * w]
+    mine = [pltpu.make_async_copy(cols(k), g.at[k, j], own_sem.at[k]) for k in range(count)]
+    make = lambda kind, k, src, slot, peer: remote(
+        src, g.at[k, slot], sends.at[kind, k], recvs.at[kind, k], "img", peer)
+    own_x = lambda k: make(0, k, cols(k), j, jx)
+    own_y = lambda k: make(1, k, cols(k), j, jy)
+    own_s = lambda k: make(2, k, cols(k), j, js)
+    diag = lambda k: make(3, k, g.at[k, jx], jx, jy) if k < mid else make(3, k, g.at[k, jy], jy, jx)
+    hand_x = lambda k: make(4, k, g.at[k, jx], jx, js)
+    hand_y = lambda k: make(5, k, g.at[k, jy], jy, js)
+    hand_d = lambda k: make(6, k, g.at[k, jd], jd, js)
+    yk = lambda t: (t + mid) % count
+
+    p_ref[...] = jnp.zeros_like(p_ref)
+    ahead = 2
+    for t in range(ahead):
+        own_x(t).start()
+        own_y(yk(t)).start()
+
+    def finish(k):
+        diag(k).wait_recv()
+        hand_d(k).start()
+
+    def project(k):
+        mine[k].wait()
+        for kind in (2, 4, 5, 6):
+            make(kind, k, cols(k), js, js).wait_recv()
+        full = g[k].reshape(ni * own, w)
+        p_ref[...] += jnp.dot(full, b[k * w:(k + 1) * w], preferred_element_type=jnp.float32)
+
+    for t in range(count):
+        k, l = t, yk(t)
+        mine[t].start()
+        own_s(t).start()
+        make(0, k, cols(k), jx, jx).wait_recv()
+        if t < mid:
+            diag(k).start()
+        hand_x(k).start()
+        make(1, l, cols(l), jy, jy).wait_recv()
+        if t < mid:
+            diag(l).start()
+        hand_y(l).start()
+        if t + ahead < count:
+            own_x(k).wait_send()
+            own_x(k + ahead).start()
+            own_y(l).wait_send()
+            own_y(yk(t + ahead)).start()
+        if t == 0:
+            compute()
+            bcopy.wait()
+        if 2 <= t < mid + 2:
+            finish(t - 2)
+            finish(t - 2 + mid)
+        if t > mid:
+            project(t - mid - 1)
+            project(t - 1)
+    project(mid - 1)
+    project(count - 1)
+
+    def drain():
+        for k in range(count):
+            if k >= count - ahead:
+                own_x(k).wait_send()
+            if k in (yk(count - 2), yk(count - 1)):
+                own_y(k).wait_send()
+            for c in (own_s(k), diag(k), hand_x(k), hand_y(k), hand_d(k)):
+                c.wait_send()
+    return drain
+
+
+def tail(nf, ni, fused, *refs):
+    if fused:
+        feat_ref, pin_ref, po_ref, cen_ref, lab_ref, cg_ref, eg_ref, *refs = refs
+        p_ref, g, b, own_sem, b_sem, gs, gr, *refs = refs
+    else:
+        p_ref, po_ref, cen_ref, lab_ref, cg_ref, eg_ref, *refs = refs
+    (z1, po, h, lab, u, emb, eo, clow, cosb, tp, tz, msg, rs, zs, zr, uq,
+         s1, r1, s2, r2, sl, rl, s4, r4, se, re, s5, r5, s6, r6, s7, r7, s8, r8, sp, rp) = refs
     f, j = lax.axis_index("feat"), lax.axis_index("img")
     images, cols = p_ref.shape
     rows = images // nf
@@ -59,11 +146,22 @@
         sent.extend(out)
         return out
 
+    outs = to_feat(lambda g: po_ref, lambda d: po.at[f], sp, rp)
+    labs = to_img(lambda c: lab_ref, lambda d: lab.at[d], sl, rl)
+
+    def prepare():
+        po[f] = po_ref[...]
+        lab[0] = lab_ref[...]
+        wide = cen_ref[...].astype(jnp.float32)
+        cinv = lax.rsqrt(jnp.sum(wide * wide, axis=1, keepdims=True) + norm_eps)
+        clow[...] = (wide * cinv).astype(jnp.bfloat16)
+
+    if fused:
+        drain = gather_project(j, ni, feat_ref, pin_ref, p_ref, g, b, own_sem, b_sem, gs, gr, prepare)
+    else:
+        prepare()
+
     first = to_feat(lambda g: p_ref.at[pl.ds(pl.multiple_of(g * rows, rows), rows)], lambda d: z1.at[d], s1, r1)
-    labs = to_img(lambda c: lab_ref, lambda d: lab.at[d], sl, rl)
-    wide = cen_ref[...].astype(jnp.float32)
-    cinv = lax.rsqrt(jnp.sum(wide * wide, axis=1, keepdims=True) + norm_eps)
-    clow[...] = (wide * cinv).astype(jnp.bfloat16)
     hid = p_ref[pl.ds(pl.multiple_of(f * rows, rows), rows)]
     for d in range(1, nf):
         first[d - 1].wait_recv()
@@ -72,10 +170,17 @@
 
     for c in to_img(lambda c: h.at[0], lambda d: h.at[d], s2, r2):
         c.wait_recv()
+    for d in range(1, nf):
+        back = lax.rem(f - d + nf, nf)
+        remote(po.at[back], po.at[back], sp.at[d], rp.at[d], "feat", zpeer(d)).wait_recv()
     embed = jnp.zeros((rows, width), jnp.float32)
+    depth = po_ref.shape[0]
     for c in range(ni):
         slot = lax.rem(j - c + ni, ni)
-        embed = embed + jnp.dot(h[slot], po_ref[c], preferred_element_type=jnp.float32)
+        at = (c * cols) % depth
+        embed = embed + jnp.dot(
+            h[slot], po[(c * cols) // depth, at:at + cols], preferred_element_type=jnp.float32
+        )
     emb[...] = embed
     inverse = lax.rsqrt(jnp.sum(embed * embed, axis=1, keepdims=True) + norm_eps)
     u[f] = (embed * inverse).astype(jnp.bfloat16)
@@ -96,16 +201,13 @@
         remote(u.at[back], u.at[back], s4.at[d], r4.at[d], "feat", zpeer(d)).wait_recv()
     for c in labs:
         c.wait_recv()
-    label = lab_ref[...]
-    for d in range(1, ni):
-        label = label + lab[d]
-    label = label[:1]
+    label = jnp.concatenate([lab[lax.rem(j - c + ni, ni)][:1] for c in range(ni)], axis=1)
 
     allu = u[...].reshape(images, width)
     cosine = lax.dot_general(clow[...], allu, (((1,), (1,)), ((), ())), preferred_element_type=jnp.float32)
     cen_rows = cen_ref.shape[0]
     begin = (f * ni + j) * cen_rows
-    cos_m, sin_m = trig_ref[0], trig_ref[1]
+    cos_m, sin_m = math.cos(margin_angle), math.sin(margin_angle)
 
     def forms(cosine):
         position = begin + lax.broadcasted_iota(jnp.int32, cosine.shape, 0)
@@ -174,6 +276,8 @@
 
     for c in sent:
         c.wait_send()
+    if fused:
+        drain()
 
     @pl.when(home)
     def _():
@@ -181,23 +285,44 @@
             remote(emb.at[pl.ds(offset, own)], eo, se.at[d], re, "feat", zpeer(d)).wait_send()
 
 
-def run_tail(nf, ni, local_cols, all_out, centres, lab_rows, trig):
-    images, cols = local_cols.shape
+def chunks_of(width):
+    for count in (12, 10, 8, 6, 4, 2):
+        if width % (count * 128) == 0:
+            return count
+    return 0
+
+
+def run_tail(nf, ni, firsts, proj_out, centres, lab_rows):
+    fused = len(firsts) == 2
+    own = lab_rows.shape[1]
+    images = own * ni
+    cols = firsts[-1].shape[1]
     cen_rows, width = centres.shape
-    rows, own, part = images // nf, images // ni, width // nf
+    rows, part = images // nf, width // nf
     f32, bf16 = jnp.float32, jnp.bfloat16
     dma = pltpu.SemaphoreType.DMA
     vm = pl.BlockSpec(memory_space=pltpu.VMEM)
+    hbm = pl.BlockSpec(memory_space=pl.ANY)
+    scratch = []
+    if fused:
+        count = chunks_of(firsts[0].shape[1])
+        scratch = [
+            pltpu.VMEM((images, cols), f32),
+            pltpu.VMEM((count, ni, own, firsts[0].shape[1] // count), bf16),
+            pltpu.VMEM(firsts[1].shape, bf16),
+            dma((count,)), dma(()), dma((7, count)), dma((7, count)),
+        ]
     return pl.pallas_call(
-        functools.partial(tail, nf, ni),
+        functools.partial(tail, nf, ni, fused),
         out_shape=(
             jax.ShapeDtypeStruct((cen_rows, width), f32),
             jax.ShapeDtypeStruct((own, part), f32),
         ),
-        in_specs=[vm, vm, vm, vm, pl.BlockSpec(memory_space=pltpu.SMEM)],
+        in_specs=([hbm, hbm] if fused else [vm]) + [vm, vm, vm],
         out_specs=(vm, vm),
-        scratch_shapes=[
+        scratch_shapes=scratch + [
             pltpu.VMEM((nf, rows, cols), f32),
+            pltpu.VMEM((nf,) + proj_out.shape, bf16),
             pltpu.VMEM((ni, rows, cols), bf16),
             pltpu.VMEM((ni,) + lab_rows.shape, jnp.int32),
             pltpu.VMEM((nf, rows, width), bf16),
@@ -221,29 +346,23 @@
             dma((nf,)), dma((nf,)),
             dma((ni,)), dma((ni,)),
             dma((nf,)), dma((nf,)),
+            dma((nf,)), dma((nf,)),
         ],
         compiler_params=pltpu.CompilerParams(
-            collective_id=1, has_side_effects=True, vmem_limit_bytes=48 * 1024 * 1024
+            collective_id=1, has_side_effects=True, vmem_limit_bytes=56 * 1024 * 1024
         ),
-    )(local_cols, all_out, centres, lab_rows, trig)
+    )(*firsts, proj_out, centres, lab_rows)
 
 
 def per_device(features, proj_in, proj_out, centres, labels):
     nf, ni = lax.axis_size("feat"), lax.axis_size("img")
-    own = labels.shape[0]
-    local_cols = jnp.dot(
-        lax.all_gather(features, "img", axis=0, tiled=True),
-        proj_in,
-        preferred_element_type=jnp.float32,
-    )
-    all_out = lax.all_gather(proj_out, "feat", axis=0, tiled=True)
-    all_out = all_out.reshape(ni, all_out.shape[0] // ni, all_out.shape[1])
-    lab_row = lax.dynamic_update_slice(
-        jnp.zeros((own * ni,), jnp.int32), labels, (lax.axis_index("img") * own,)
-    )
-    lab_rows = jnp.broadcast_to(lab_row[None], (8, own * ni))
-    trig = jnp.stack([jnp.cos(jnp.float32(margin_angle)), jnp.sin(jnp.float32(margin_angle))])
-    return run_tail(nf, ni, local_cols, all_out, centres, lab_rows, trig)
+    if ni == 2 * 2 * 2 and chunks_of(features.shape[1]):
+        firsts = (features, proj_in)
+    else:
+        everything = lax.all_gather(features, "img", axis=0, tiled=True)
+        firsts = (jnp.dot(everything, proj_in, preferred_element_type=jnp.float32),)
+    lab_rows = jnp.broadcast_to(labels[None], (8, labels.shape[0]))
+    return run_tail(nf, ni, firsts, proj_out, centres, lab_rows)
 
 
 def solution(mesh):

time: 157 us -> 130 us (0.83)
  Pallas kernels: 51.4 us -> 118 us
  waiting for transfers between devices: 59.7 us -> 0 us
  blocking collectives: 21.8 us -> 0 us
  between operations: 14.1 us -> 0.64 us
  local copies, waits for them, and re-layouts: 2.57 us -> 10.5 us
  matrix products: 6.92 us -> 0 us
    pallas_call x1, Pallas kernels: 51.4 us -> 118 us  [run_tail(): pl.pallas_call(functools.partial(tail, nf, ni, fused), out_shape=(jax.Sha...]
    all_gather x1 -> x0, waiting for transfers between devices: 59.1 us -> none  [per_device(): lax.all_gather(features, 'img', axis=0, tiled=True)]
    all_gather x1 -> x0, blocking collectives: 21.8 us -> none  [per_device(): all_out = lax.all_gather(proj_out, 'feat', axis=0, tiled=True)]
    unnamed x10 -> x3, local copies, waits for them, and re-layouts: 1.6 us -> 9.26 us
    dot_general x1 -> x0, matrix products: 6.92 us -> none  [per_device(): jnp.dot(lax.all_gather(features, 'img', axis=0, tiled=True), proj_in, pre...]
  transfers between devices with their start and end apart: 1 -> 0, of which waited for: 1 -> 0; matrix products, arithmetic and copies ran while one was open for 1% -> 0% of each run, Pallas kernels for 0% -> 0%
where the time goes in v2:
time: 130 us; the launch traced here: 129 us
  Pallas kernels  118 us (91%)
  local copies, waits for them, and re-layouts  10.5 us (8%)
    pallas_call x1, Pallas kernels, run_tail(): pl.pallas_call(functools.partial(tail, nf, ni, fused), out_shape=(jax.Sha...  118 us
    unnamed x3, local copies, waits for them, and re-layouts  9.26 us

profile of v2, /device:TPU:0, one launch (start us, length us, event | category | flops | bytes accessed | tf_op | source)
XLA Modules:
  0.0 129.2 jit_solution(2056174466883402679)
XLA Ops:
  0.6 1.2 broadcast_in_dim.2.refs_4_
  1.9 5.6 %copy.7.refs_1_ = bf16[15360,96]{1,0:T(8,128)(2,1)} copy(bf16[15360,96]{0,1:T(8,128)(2,1)} %param.6) | data formatting | bytes 5898240 | tf_op args[1]
  7.5 118.1 %shard_map.68 = (f32[512,512]{1,0:T(8,128)}, f32[56,128]{1,0:T(8,128)}) custom-call(bf16[56,15360]{1,0:T(8,128)(2,1)} %refs_0_.1, bf16[15360,96]{1,0:T(8,128)(2,1)} %copy.7.refs_1_, bf16[192,512]{1,0:T(8,128)(2,1)} %refs_2_.1, bf16[512,512]{1,0:T(8,128)(2,1)} %refs_3_.1, s32[8,56]{1,0:T(8,128)} %broadcast_in_dim.2.refs_4_), custom_call_target="tpu_custom_call" | custom-call | tf_op jit(solution)/shard_map/pallas_call | solution.py:315
  125.6 2.3 %copy.10 = f32[512,512]{1,0:T(8,128)} copy(f32[512,512]{1,0:T(8,128)} %get-tuple-element.4) | data formatting | bytes 2097152
  127.9 1.4 %copy.11 = f32[56,128]{1,0:T(8,128)} copy(f32[56,128]{1,0:T(8,128)} %get-tuple-element.5) | data formatting | bytes 57344

commit v3 on v2

--- a/solution.py
+++ b/solution.py
@@ -109,7 +109,7 @@
     else:
         p_ref, po_ref, cen_ref, lab_ref, cg_ref, eg_ref, *refs = refs
     (z1, po, h, lab, u, emb, eo, clow, cosb, tp, tz, msg, rs, zs, zr, uq,
-         s1, r1, s2, r2, sl, rl, s4, r4, se, re, s5, r5, s6, r6, s7, r7, s8, r8, sp, rp) = refs
+         s1, r1, s2, r2, sl, rl, s4, r4, se, re, s5, r5, s6, r6, s7, r7, s8, r8, sp, rp, sh, rh) = refs
     f, j = lax.axis_index("feat"), lax.axis_index("img")
     images, cols = p_ref.shape
     rows = images // nf
@@ -183,9 +183,22 @@
         )
     emb[...] = embed
     inverse = lax.rsqrt(jnp.sum(embed * embed, axis=1, keepdims=True) + norm_eps)
-    u[f] = (embed * inverse).astype(jnp.bfloat16)
-
-    units = to_feat(lambda g: u.at[f], lambda d: u.at[f], s4, r4)
+
+    side = lax.rem(j, 2)
+    half = width // 2
+    low = (embed * inverse).astype(jnp.bfloat16)
+    u[0, f] = low[:, :half]
+    u[1, f] = low[:, half:]
+    units = to_feat(lambda g: u.at[side, f], lambda d: u.at[side, f], s4, r4)
+    sibling = j + 1 - 2 * side
+    hands = []
+    for d in range(1, nf):
+        back = lax.rem(f - d + nf, nf)
+        remote(u.at[side, back], u.at[side, back], s4.at[d], r4.at[d], "feat", zpeer(d)).wait_recv()
+        c = remote(u.at[side, back], u.at[side, back], sh.at[d], rh.at[d], "img", sibling)
+        c.start()
+        hands.append(c)
+    sent.extend(hands)
     holder = (j * own) // rows
     offset = pl.multiple_of(lax.rem(j * own, rows), own)
     home = f == holder
@@ -198,12 +211,12 @@
 
     for d in range(1, nf):
         back = lax.rem(f - d + nf, nf)
-        remote(u.at[back], u.at[back], s4.at[d], r4.at[d], "feat", zpeer(d)).wait_recv()
+        remote(u.at[1 - side, back], u.at[1 - side, back], sh.at[d], rh.at[d], "img", sibling).wait_recv()
     for c in labs:
         c.wait_recv()
     label = jnp.concatenate([lab[lax.rem(j - c + ni, ni)][:1] for c in range(ni)], axis=1)
 
-    allu = u[...].reshape(images, width)
+    allu = jnp.concatenate([u[0].reshape(images, half), u[1].reshape(images, half)], axis=1)
     cosine = lax.dot_general(clow[...], allu, (((1,), (1,)), ((), ())), preferred_element_type=jnp.float32)
     cen_rows = cen_ref.shape[0]
     begin = (f * ni + j) * cen_rows
@@ -238,7 +251,6 @@
     dcos = (dlogit * scale_logit * jnp.where(target, slope, 1.0)).astype(jnp.bfloat16)
 
     terms = lax.dot_general(dcos, clow[...], (((0,), (0,)), ((), ())), preferred_element_type=jnp.float32)
-    half = width // 2
     for c in range(ni):
         block = terms[c * own:(c + 1) * own]
         msg[c] = jnp.concatenate([block[:, :half], block[:, half:]], axis=0).astype(jnp.bfloat16)
@@ -325,7 +337,7 @@
             pltpu.VMEM((nf,) + proj_out.shape, bf16),
             pltpu.VMEM((ni, rows, cols), bf16),
             pltpu.VMEM((ni,) + lab_rows.shape, jnp.int32),
-            pltpu.VMEM((nf, rows, width), bf16),
+            pltpu.VMEM((2, nf, rows, width // 2), bf16),
             pltpu.VMEM((rows, width), f32),
             pltpu.VMEM((own, width), f32),
             pltpu.VMEM((cen_rows, width), bf16),
@@ -345,6 +357,7 @@
             dma((ni,)), dma((ni,)),
             dma((nf,)), dma((nf,)),
             dma((ni,)), dma((ni,)),
+            dma((nf,)), dma((nf,)),
             dma((nf,)), dma((nf,)),
             dma((nf,)), dma((nf,)),
         ],

time: 130 us -> 121 us (0.931)
  Pallas kernels: 118 us -> 109 us
    pallas_call x1, Pallas kernels: 118 us -> 109 us  [run_tail(): pl.pallas_call(functools.partial(tail, nf, ni, fused), out_shape=(jax.Sha...]
where the time goes in v3:
time: 121 us
  Pallas kernels  109 us (90%)
  local copies, waits for them, and re-layouts  10.5 us (9%)
    pallas_call x1, Pallas kernels, run_tail(): pl.pallas_call(functools.partial(tail, nf, ni, fused), out_shape=(jax.Sha...  109 us
    unnamed x3, local copies, waits for them, and re-layouts  9.26 us

profile of v3, /device:TPU:0, one launch (start us, length us, event | category | flops | bytes accessed | tf_op | source)
XLA Modules:
  0.0 120.5 jit_solution(17281488896741755194)
XLA Ops:
  0.6 1.2 %broadcast_in_dim.2.refs_4_ = s32[8,56]{1,0:T(8,128)} broadcast(s32[56]{0:T(128)} %param.9), dimensions={1} | broadcast | bytes 2016 | tf_op jit(solution)/shard_map/broadcast_in_dim | solution.py:377
  1.9 5.6 %copy.7.refs_1_ = bf16[15360,96]{1,0:T(8,128)(2,1)} copy(bf16[15360,96]{0,1:T(8,128)(2,1)} %param.6) | data formatting | bytes 5898240 | tf_op args[1]
  7.5 109.4 %shard_map.68 = (f32[512,512]{1,0:T(8,128)}, f32[56,128]{1,0:T(8,128)}) custom-call(bf16[56,15360]{1,0:T(8,128)(2,1)} %refs_0_.1, bf16[15360,96]{1,0:T(8,128)(2,1)} %copy.7.refs_1_, bf16[192,512]{1,0:T(8,128)(2,1)} %refs_2_.1, bf16[512,512]{1,0:T(8,128)(2,1)} %refs_3_.1, s32[8,56]{1,0:T(8,128)} %broadcast_in_dim.2.refs_4_), custom_call_target="tpu_custom_call" | custom-call | tf_op jit(solution)/shard_map/pallas_call | solution.py:327
  116.9 2.3 %copy.10 = f32[512,512]{1,0:T(8,128)} copy(f32[512,512]{1,0:T(8,128)} %get-tuple-element.4) | data formatting | bytes 2097152
  119.2 1.4 %copy.11 = f32[56,128]{1,0:T(8,128)} copy(f32[56,128]{1,0:T(8,128)} %get-tuple-element.5) | data formatting | bytes 57344
